TPU v7x, 128 devices: a whole 4x4x4 slice. The times are simulated.
128 devices in a mesh: seq: 16 (over y, z_lo, core), tp: 4 (over x), rep: 2 (over z_hi).
Axes of the slice: x: 4, y: 4, z: 4 (z_hi: 2, z_lo: 2; z = z_hi * 2 + z_lo), core: 2. Of those that a mesh axis runs over, the one named last changes fastest.
Arguments:
- tokens: bfloat16 [2, 12288, 3072], P('rep', 'seq'), may hold values from -6 to 6
- in_panels: bfloat16 [3072, 4, 4096], P(('seq', 'rep'), None, 'tp'), may hold values from -0.109375 to 0.109375
- out_panel: bfloat16 [4096, 3072], P('tp', ('seq', 'rep')), may hold values from -0.09375 to 0.09375
- decay_power: int32 [32], P('tp'), may hold values from 0 to 8
- boundary: int32 [2], P('rep'), may hold values from 1 to 12287
Outputs:
- layer_out: bfloat16 [2, 12288, 3072], P('rep', 'seq', 'tp')
All inputs are finite; a program needn't handle non-finite values.
Results may differ from a plain program's by a relative error of at most 0.019.
Values may be sent and summed in bfloat16 or wider, within the bound.
A program may use at most 128 MiB of HBM per device.

v0:
```python
import jax
import jax.numpy as jnp
from jax import lax
from jax.sharding import PartitionSpec as P

D = 3072
HDIM = 128
log_half = -0.6931471805599453
epsilon = 1e-06


def attend_block(queries, key_rows, val_rows, log_rate, anchor, prompt_start):
    extent = queries.shape[0]
    positions = anchor + jnp.arange(extent, dtype=jnp.int32)
    newer_mask = positions >= prompt_start
    offsets = (positions[:, None] - positions[None, :]).astype(jnp.float32)
    allowed = (offsets >= 0.0) & (newer_mask[:, None] == newer_mask[None, :])
    weights = jnp.where(
        allowed[None], jnp.exp(log_rate[:, None, None] * jnp.maximum(offsets, 0.0)[None]), 0.0
    )
    scores = jnp.einsum("ihd,jhd->hij", queries, key_rows, preferred_element_type=jnp.float32)
    scores = (scores * weights).astype(jnp.bfloat16)
    within = jnp.einsum("hij,jhd->ihd", scores, val_rows, preferred_element_type=jnp.float32)
    final_pos = anchor + extent - 1
    kept_rows = (newer_mask == (final_pos >= prompt_start)).astype(jnp.float32)
    steps_out = (final_pos - positions).astype(jnp.float32)
    key_scale = jnp.exp(log_rate[None, :] * steps_out[:, None]) * kept_rows[:, None]
    decayed = (key_rows.astype(jnp.float32) * key_scale[:, :, None]).astype(jnp.bfloat16)
    local_state = jnp.einsum("jhd,jhe->hde", decayed, val_rows, preferred_element_type=jnp.float32)
    return (within, local_state)


def local(tokens, in_panels, out_panel, decay_power, boundary):
    slab_rows = tokens[0]
    extent = slab_rows.shape[0]
    seq_count = lax.axis_size("seq")
    own_index = lax.axis_index("seq")
    anchor = own_index * extent
    prompt_start = boundary[0]
    log_rate = log_half * jnp.exp2(decay_power.astype(jnp.float32)) / (extent * seq_count)
    head_count = decay_power.shape[0]
    width = in_panels.shape[2]
    flat_in = lax.optimization_barrier(in_panels.reshape(in_panels.shape[0], 4 * width))
    full_in = lax.all_gather(flat_in, ("seq", "rep"), axis=0, tiled=True)
    full_out = lax.all_gather(out_panel.T, ("seq", "rep"), axis=0, tiled=True)
    projected = jnp.dot(slab_rows, full_in, preferred_element_type=jnp.float32)
    projected = lax.optimization_barrier(projected)
    projected = projected.reshape(extent, 4, head_count, HDIM)
    queries = (jax.nn.silu(projected[:, 0]) * HDIM ** (-0.5)).astype(jnp.bfloat16)
    key_rows = jax.nn.silu(projected[:, 1]).astype(jnp.bfloat16)
    val_rows = projected[:, 2].astype(jnp.bfloat16)
    gate_rows = jax.nn.sigmoid(projected[:, 3])
    within, local_state = attend_block(queries, key_rows, val_rows, log_rate, anchor, prompt_start)
    states = lax.all_gather(local_state.astype(jnp.bfloat16), "seq")
    owners = jnp.arange(seq_count, dtype=jnp.int32)
    between = (own_index - 1 - owners).astype(jnp.float32)
    crossing = prompt_start // extent
    reaches = (owners < own_index) & ~((owners < crossing) & (crossing < own_index))
    carry = jnp.where(
        reaches[:, None],
        jnp.exp(log_rate[None, :] * extent * jnp.maximum(between, 0.0)[:, None]),
        0.0,
    )
    prior_state = jnp.sum(carry[:, :, None, None] * states.astype(jnp.float32), axis=0)
    attended = within
    positions = anchor + jnp.arange(extent, dtype=jnp.int32)
    use_prior = ((positions < prompt_start) | (anchor > prompt_start)).astype(jnp.float32)
    steps_in = jnp.arange(1, extent + 1, dtype=jnp.int32).astype(jnp.float32)
    query_scale = jnp.exp(log_rate[None, :] * steps_in[:, None]) * use_prior[:, None]
    scaled = queries.astype(jnp.float32) * query_scale[:, :, None]
    attended = attended + jnp.einsum(
        "ihd,hde->ihe", scaled, prior_state, precision=lax.Precision.HIGHEST
    )
    square = jnp.mean(attended * attended, axis=-1, keepdims=True)
    gated_rows = (
        (attended * lax.rsqrt(square + epsilon) * gate_rows)
        .astype(jnp.bfloat16)
        .reshape(extent, head_count * HDIM)
    )
    head_partial = lax.dot_general(
        gated_rows, full_out, (((1,), (1,)), ((), ())), preferred_element_type=jnp.float32
    )
    summed = lax.psum_scatter(
        head_partial.astype(jnp.bfloat16), "tp", scatter_dimension=1, tiled=True
    )
    return summed[None]


def solution(mesh):
    return jax.shard_map(
        local,
        mesh=mesh,
        in_specs=(
            P("rep", "seq", None),
            P(("seq", "rep"), None, "tp"),
            P("tp", ("seq", "rep")),
            P("tp"),
            P("rep"),
        ),
        out_specs=P("rep", "seq", "tp"),
        check_vma=False,
    )
```

profile of v0, /device:TPU:1, one launch (start us, length us, event | category | flops | bytes accessed | tf_op | source)
XLA Modules:
  0.0 410.5 jit_solution(10307200429481321164)
XLA Ops:
  6.5 0.0 all-gather.5.cloned.1.call-start
  6.5 2.3 copy.26
  8.8 0.0 all-gather.5.cloned.1.call-update
  8.8 0.0 all-gather.9.cloned.1.call-start
  9.6 0.7 broadcast_multiply_fusion
  10.3 0.1 exponential_multiply_fusion
  10.4 145.5 %all-gather.5.cloned.1.call-done = bf16[3072,4096]{1,0:T(8,128)(2,1)} async-done(((bf16[96,4096]{1,0:T(8,128)(2,1)}), bf16[3072,4096]{1,0:T(8,128)(2,1)}) %all-gather.5.cloned.1.call-update) | async-done | bytes 25165840 | tf_op jit(solution)/shard_map/all_gather | solution.py:44
  155.9 26.0 %fusion.5 = f32[768,4096]{1,0:T(8,128)} fusion(bf16[3072,4096]{1,0:T(8,128)(2,1)} %all-gather.5.cloned.1.call-done, bf16[1,768,3072]{2,1,0:T(8,128)(2,1)} %param.5), kind=kOutput, calls=%fused_computation.7 | convolution fusion | flops 19327352832 | bytes 42467328 | tf_op jit(solution)/shard_map/dot_general | solution.py:46
  181.9 12.0 %copy.27 = f32[96,8,32,128]{3,2,1,0:T(8,128)} copy(f32[96,8,32,128]{3,1,2,0:T(8,128)} %bitcast.65) | data formatting | bytes 25165824
  193.9 7.0 %fusion.31 = (f32[768,1,8,128]{3,2,1,0:T(8,128)S(1)}, f32[768,1,8,128]{3,2,1,0:T(8,128)}, f32[768,1,8,128]{3,2,1,0:T(8,128)}) fusion(f32[768,4,8,128]{3,2,1,0:T(8,128)} %bitcast.63), kind=kLoop, calls=%fused_computation.52 | loop fusion | bytes 18874368 | tf_op jit(solution)/shard_map/slice | solution.py:52
  200.9 3.2 slice.17
  204.1 2.9 copy.24
  207.0 4.9 %fusion.21 = bf16[8,128,128]{2,1,0:T(8,128)(2,1)} fusion(f32[768,8]{0,1:T(8,128)S(1)} %get-tuple-element.9, bf16[768,1,8,128]{0,3,2,1:T(8,128)(2,1)} %copy.24, f32[768,1,8,128]{3,2,1,0:T(8,128)} %get-tuple-element.7), kind=kOutput, calls=%fused_computation.31 | convolution fusion | flops 207749120 | bytes 5005312 | tf_op jit(solution)/shard_map/jhd,jhe->hde/dot_general | solution.py:29
  211.9 0.0 all-gather.9.cloned.1.call-update
  212.0 0.0 all-gather.7.cloned.1.call-start
  212.0 0.7 all-gather.7.cloned.1.call-update
  212.7 0.0 reduce-scatter.2.cloned.1.call-start
  212.8 0.1 exponential_select_fusion
  212.9 1.5 fusion.12
  214.4 1.8 convert_maximum_fusion
  216.1 2.5 copy.25
  218.6 13.7 %fusion = f32[8,128,768]{2,1,0:T(8,128)} fusion(f32[768,768]{1,0:T(8,128)} %convert_maximum_fusion, f32[8]{0:T(128)S(1)} %get-tuple-element.11, pred[768,768]{1,0:T(8,128)(4,1)} %fusion.12, bf16[768,1,8,128]{0,3,2,1:T(8,128)(2,1)} %copy.24, f32[768,1,8,128]{3,2,1,0:T(8,128)} %get-tuple-element.7, f32[768,1,8,128]{3,2,1,0:T(8,128)} %get-tuple-element.6), kind=kOutput, calls=%fused_computation.1 | convolution fusion | flops 2443444224 | bytes 13959200 | tf_op jit(solution)/shard_map/hij,jhd->ihd/dot_general | solution.py:23
  232.3 18.1 %all-gather.9.cloned.1.call-done = bf16[128,128,128]{2,1,0:T(8,128)(2,1)} async-done(((bf16[8,128,128]{2,1,0:T(8,128)(2,1)}), bf16[128,128,128]{2,1,0:T(8,128)(2,1)}) %all-gather.9.cloned.1.call-update) | async-done | bytes 4194320 | tf_op jit(solution)/shard_map/all_gather | solution.py:54
  250.4 3.1 fusion.2
  253.5 0.0 copy-done.1
  253.5 0.0 copy-start
  253.5 8.0 %fusion.8 = (f32[768,8]{0,1:T(8,128)S(1)}, f32[8,128,768]{2,1,0:T(8,128)S(1)}) fusion(f32[8,128,768]{2,1,0:T(8,128)} %fusion, f32[8,128,128]{2,1,0:T(8,128)S(1)} %fusion.2, f32[768,8]{0,1:T(8,128)S(1)} %get-tuple-element.8, f32[768,1,8,128]{3,2,1,0:T(8,128)S(1)} %copy-done.1), kind=kOutput, calls=%fused_computation.15 | convolution fusion | flops 1216604160 | bytes 10010624 | tf_op jit(solution)/shard_map/ihd,hde->ihe/dot_general | solution.py:71
  261.5 0.9 fusion.7
  262.4 79.6 %all-gather.7.cloned.1.call-done = bf16[3072,1024]{1,0:T(8,128)(2,1)} async-done(((bf16[96,1024]{1,0:T(8,128)(2,1)}), bf16[3072,1024]{1,0:T(8,128)(2,1)}) %all-gather.7.cloned.1.call-update) | async-done | bytes 6291472 | tf_op jit(solution)/shard_map/all_gather | solution.py:45
  342.0 9.7 %convolution_convert_fusion = bf16[768,3072]{1,0:T(8,128)(2,1)} fusion(bf16[768,1024]{0,1:T(8,128)(2,1)S(1)} %bitcast.68, bf16[3072,1024]{1,0:T(8,128)(2,1)} %all-gather.7.cloned.1.call-done), kind=kOutput, calls=%fused_computation.6 | convolution fusion | flops 4834197504 | bytes 12582912 | tf_op jit(solution)/shard_map/dot_general | solution.py:80
  351.7 0.0 reduce-scatter.2.cloned.1.call-update
  351.7 52.3 %reduce-scatter.2.cloned.1.call-done = bf16[768,768]{1,0:T(8,128)(2,1)} async-done(((bf16[768,3072]{1,0:T(8,128)(2,1)}), bf16[768,768]{1,0:T(8,128)(2,1)}) %reduce-scatter.2.cloned.1.call-update) | async-done | bytes 1179664 | tf_op jit(solution)/shard_map/reduce_scatter | solution.py:83
  (9 shorter events, 0.1 us)
Async XLA Ops:
  6.5 149.4 %all-gather.5.cloned.1.call-start = ((), (), s32[]{:S(2)}) async-start(), calls=%async_computation.1 | async-start | bytes 25952256 | tf_op jit(solution)/shard_map/all_gather | solution.py:44
  8.8 241.5 %all-gather.9.cloned.1.call-start = ((), (), s32[]{:S(2)}) async-start(), calls=%async_computation.4 | async-start | bytes 4456448 | tf_op jit(solution)/shard_map/all_gather | solution.py:54
  212.0 130.0 %all-gather.7.cloned.1.call-start = ((), (), s32[]{:S(2)}) async-start(), calls=%async_computation.2 | async-start | bytes 6488064 | tf_op jit(solution)/shard_map/all_gather | solution.py:45
  212.7 191.3 %reduce-scatter.2.cloned.1.call-start = ((), (), s32[]{:S(2)}) async-start(), calls=%async_computation.3 | async-start | bytes 5898240 | tf_op jit(solution)/shard_map/reduce_scatter | solution.py:83
  232.3 21.2 %copy-start.1 = (f32[768,1,8,128]{3,2,1,0:T(8,128)S(1)}, f32[768,1,8,128]{3,2,1,0:T(8,128)}, u32[]{:S(2)}) copy-start(f32[768,1,8,128]{3,2,1,0:T(8,128)} %get-tuple-element.6) | copy-start | bytes 9437188
  253.5 8.0 %copy-start = (f32[768,1,8,128]{0,3,2,1:T(8,128)S(1)}, f32[768,1,8,128]{0,3,2,1:T(8,128)}, u32[]{:S(2)}) copy-start(f32[768,1,8,128]{0,3,2,1:T(8,128)} %copy.25) | copy-start | bytes 9437188
Sparse Core Ops, SparseCore 0:
  9.0 146.8 all-gather.4
  212.1 38.2 all-gather.8
  252.1 89.8 all-gather.6
  351.8 52.0 reduce-scatter.1
where the time goes:
time: 411 us; the launch traced here: 410 us
  waiting for transfers between devices  296 us (72%)
  matrix products  62.3 us (15%)
  local copies, waits for them, and re-layouts  29.8 us (7%)
  between operations  13.9 us (3%)
  other arithmetic  8.14 us (2%)
    all_gather x1, waiting for transfers between devices, local(): full_in = lax.all_gather(flat_in, ('seq', 'rep'), axis=0, tiled=True)  146 us
    all_gather x1, waiting for transfers between devices, local(): full_out = lax.all_gather(out_panel.T, ('seq', 'rep'), axis=0, tiled=True)  79.6 us
    reduce_scatter x1, waiting for transfers between devices, local(): lax.psum_scatter(head_partial.astype(jnp.bfloat16), 'tp', scatter_dimensi...  52.3 us
    dot_general x1, matrix products, local(): projected = jnp.dot(slab_rows, full_in, preferred_element_type=jnp.float32)  26 us
    unnamed x8, local copies, waits for them, and re-layouts  19.6 us
    all_gather x1, waiting for transfers between devices, local(): states = lax.all_gather(local_state.astype(jnp.bfloat16), 'seq')  18.1 us
    dot_general x1, matrix products, attend_block(): jnp.einsum('hij,jhd->ihd', scores, val_rows, preferred_element_type=jnp.f...  13.7 us
    dot_general x1, matrix products, local(): lax.dot_general(gated_rows, full_out, (((1,), (1,)), ((), ())), preferred...  9.71 us
  transfers between devices with their start and end apart: 4, of which 4 were waited for; matrix products, arithmetic and copies ran while one was open for 8% of the time, Pallas kernels for 0%

commit v1 on v0

--- a/solution.py
+++ b/solution.py
@@ -41,7 +41,10 @@
     head_count = decay_power.shape[0]
     width = in_panels.shape[2]
     flat_in = lax.optimization_barrier(in_panels.reshape(in_panels.shape[0], 4 * width))
-    full_in = lax.all_gather(flat_in, ("seq", "rep"), axis=0, tiled=True)
+    devices = lax.axis_size(("seq", "rep"))
+    tiles = jnp.stack([flat_in for _ in range(devices)])
+    tiles = lax.all_to_all(tiles, ("seq", "rep"), split_axis=0, concat_axis=0)
+    full_in = jnp.concatenate(tiles, axis=0)
     full_out = lax.all_gather(out_panel.T, ("seq", "rep"), axis=0, tiled=True)
     projected = jnp.dot(slab_rows, full_in, preferred_element_type=jnp.float32)
     projected = lax.optimization_barrier(projected)

time: 411 us -> 690 us (1.68)
  waiting for transfers between devices: 296 us -> 559 us
  starting transfers between devices: 0.12 us -> 9.9 us
  local copies, waits for them, and re-layouts: 29.8 us -> 37.6 us
    all_to_all x0 -> x1, waiting for transfers between devices: none -> 335 us  [local(): tiles = lax.all_to_all(tiles, ('seq', 'rep'), split_axis=0, concat_axis=0)]
    all_gather x1 -> x0, waiting for transfers between devices: 146 us -> none  [local(): full_in = lax.all_gather(flat_in, ('seq', 'rep'), axis=0, tiled=True)]
    all_gather x1, waiting for transfers between devices: 18.1 us -> 91.8 us  [local(): states = lax.all_gather(local_state.astype(jnp.bfloat16), 'seq')]
    all_to_all x0 -> x1, starting transfers between devices: none -> 9.78 us  [local(): tiles = lax.all_to_all(tiles, ('seq', 'rep'), split_axis=0, concat_axis=0)]
    another operation x0 -> x1, local copies, waits for them, and re-layouts: none -> 8.63 us  [local(): tiles = jnp.stack([flat_in for _ in range(devices)])]
    unnamed x8 -> x10, local copies, waits for them, and re-layouts: 19.6 us -> 18.8 us
  transfers between devices with their start and end apart: 4 -> 4, of which waited for: 4 -> 4; matrix products, arithmetic and copies ran while one was open for 8% -> 5% of each run, Pallas kernels for 0% -> 0%
where the time goes in v1:
time: 690 us
  waiting for transfers between devices  559 us (81%)
  matrix products  62.2 us (9%)
  local copies, waits for them, and re-layouts  37.6 us (5%)
  between operations  13.9 us (2%)
  starting transfers between devices  9.9 us (1%)
  other arithmetic  7.48 us (1%)
    all_to_all x1, waiting for transfers between devices, local(): tiles = lax.all_to_all(tiles, ('seq', 'rep'), split_axis=0, concat_axis=0)  335 us
    all_gather x1, waiting for transfers between devices, local(): states = lax.all_gather(local_state.astype(jnp.bfloat16), 'seq')  91.8 us
    all_gather x1, waiting for transfers between devices, local(): full_out = lax.all_gather(out_panel.T, ('seq', 'rep'), axis=0, tiled=True)  79.5 us
    reduce_scatter x1, waiting for transfers between devices, local(): lax.psum_scatter(head_partial.astype(jnp.bfloat16), 'tp', scatter_dimensi...  52.2 us
    dot_general x1, matrix products, local(): projected = jnp.dot(slab_rows, full_in, preferred_element_type=jnp.float32)  26 us
    unnamed x10, local copies, waits for them, and re-layouts  18.8 us
  transfers between devices with their start and end apart: 4, of which 4 were waited for; matrix products, arithmetic and copies ran while one was open for 5% of the time, Pallas kernels for 0%

profile of v1, /device:TPU:1, one launch (start us, length us, event | category | flops | bytes accessed | tf_op | source)
XLA Modules:
  0.0 689.9 jit_solution(6597331146889387301)
XLA Ops:
  6.5 1.4 copy.26
  7.9 8.6 %stack.2 = bf16[32,96,4096]{2,1,0:T(8,128)(2,1)} broadcast(bf16[96,4096]{1,0:T(8,128)(2,1)S(1)} %bitcast.68), dimensions={1,2} | broadcast | bytes 25952256 | tf_op jit(solution)/shard_map/stack | solution.py:45
  16.6 9.8 %all-to-all-start = ((bf16[32,96,4096]{2,1,0:T(8,128)(2,1)}), bf16[32,96,4096]{2,1,0:T(8,128)(2,1)}, u32[]{:S(2)}, u32[]{:S(2)}) async-start(bf16[32,96,4096]{2,1,0:T(8,128)(2,1)} %stack.2), calls=%async_computation | async-start | bytes 50331648 | tf_op jit(solution)/shard_map/all_to_all | solution.py:46
  26.4 0.0 all-gather.6.cloned.1.call-start
  27.1 0.0 copy-done.2
  27.2 0.1 exponential_multiply_fusion
  27.2 334.5 %all-to-all-done = bf16[32,96,4096]{2,1,0:T(8,128)(2,1)} async-done(((bf16[32,96,4096]{2,1,0:T(8,128)(2,1)}), bf16[32,96,4096]{2,1,0:T(8,128)(2,1)}, u32[]{:S(2)}, u32[]{:S(2)}) %all-to-all-start) | async-done | bytes 25165856 | tf_op jit(solution)/shard_map/all_to_all | solution.py:46
  361.8 26.0 %fusion.5 = f32[768,4096]{1,0:T(8,128)} fusion(bf16[3072,4096]{1,0:T(8,128)(2,1)} %bitcast.1, bf16[1,768,3072]{2,1,0:T(8,128)(2,1)} %param.5), kind=kOutput, calls=%fused_computation.7 | convolution fusion | flops 19327352832 | bytes 42467328 | tf_op jit(solution)/shard_map/dot_general | solution.py:49
  387.8 12.0 %copy.27 = f32[96,8,32,128]{3,2,1,0:T(8,128)} copy(f32[96,8,32,128]{3,1,2,0:T(8,128)} %bitcast.66) | data formatting | bytes 25165824
  399.8 7.0 %fusion.31 = (f32[768,1,8,128]{3,2,1,0:T(8,128)S(1)}, f32[768,1,8,128]{3,2,1,0:T(8,128)}, f32[768,1,8,128]{3,2,1,0:T(8,128)}) fusion(f32[768,4,8,128]{3,2,1,0:T(8,128)} %bitcast.64), kind=kLoop, calls=%fused_computation.52 | loop fusion | bytes 18874368 | tf_op jit(solution)/shard_map/slice | solution.py:55
  406.8 3.2 slice.17
  410.0 2.9 copy.24
  412.9 4.9 fusion.21
  417.8 0.0 all-gather.6.cloned.1.call-update
  417.8 0.0 all-gather.4.cloned.1.call-start
  417.9 0.7 all-gather.4.cloned.1.call-update
  418.6 0.0 reduce-scatter.2.cloned.1.call-start
  418.7 0.1 exponential_select_fusion
  418.8 1.5 fusion.12
  420.3 1.8 convert_maximum_fusion
  422.0 2.5 copy.25
  424.5 13.6 %fusion = f32[8,128,768]{2,1,0:T(8,128)} fusion(f32[768,768]{1,0:T(8,128)} %convert_maximum_fusion, f32[8]{0:T(128)S(1)} %get-tuple-element.11, pred[768,768]{1,0:T(8,128)(4,1)} %fusion.12, bf16[768,1,8,128]{0,3,2,1:T(8,128)(2,1)} %copy.24, f32[768,1,8,128]{3,2,1,0:T(8,128)} %get-tuple-element.7, f32[768,1,8,128]{3,2,1,0:T(8,128)} %get-tuple-element.6), kind=kOutput, calls=%fused_computation.1 | convolution fusion | flops 2443444224 | bytes 13959200 | tf_op jit(solution)/shard_map/hij,jhd->ihd/dot_general | solution.py:23
  438.1 91.8 %all-gather.6.cloned.1.call-done = bf16[128,128,128]{2,1,0:T(8,128)(2,1)} async-done(((bf16[8,128,128]{2,1,0:T(8,128)(2,1)}), bf16[128,128,128]{2,1,0:T(8,128)(2,1)}) %all-gather.6.cloned.1.call-update) | async-done | bytes 4194320 | tf_op jit(solution)/shard_map/all_gather | solution.py:57
  529.9 3.1 fusion.2
  533.0 0.0 copy-done.1
  533.0 0.0 copy-start
  533.0 8.0 %fusion.8 = (f32[768,8]{0,1:T(8,128)S(1)}, f32[8,128,768]{2,1,0:T(8,128)S(1)}) fusion(f32[8,128,768]{2,1,0:T(8,128)} %fusion, f32[8,128,128]{2,1,0:T(8,128)S(1)} %fusion.2, f32[768,8]{0,1:T(8,128)S(1)} %get-tuple-element.8, f32[768,1,8,128]{3,2,1,0:T(8,128)S(1)} %copy-done.1), kind=kOutput, calls=%fused_computation.15 | convolution fusion | flops 1216604160 | bytes 10010624 | tf_op jit(solution)/shard_map/ihd,hde->ihe/dot_general | solution.py:74
  541.0 0.9 fusion.7
  541.9 79.5 %all-gather.4.cloned.1.call-done = bf16[3072,1024]{1,0:T(8,128)(2,1)} async-done(((bf16[96,1024]{1,0:T(8,128)(2,1)}), bf16[3072,1024]{1,0:T(8,128)(2,1)}) %all-gather.4.cloned.1.call-update) | async-done | bytes 6291472 | tf_op jit(solution)/shard_map/all_gather | solution.py:48
  621.4 9.7 %convolution_convert_fusion = bf16[768,3072]{1,0:T(8,128)(2,1)} fusion(bf16[768,1024]{0,1:T(8,128)(2,1)S(1)} %bitcast.69, bf16[3072,1024]{1,0:T(8,128)(2,1)} %all-gather.4.cloned.1.call-done), kind=kOutput, calls=%fused_computation.6 | convolution fusion | flops 4834197504 | bytes 12582912 | tf_op jit(solution)/shard_map/dot_general | solution.py:83
  631.1 0.0 reduce-scatter.2.cloned.1.call-update
  631.1 52.2 %reduce-scatter.2.cloned.1.call-done = bf16[768,768]{1,0:T(8,128)(2,1)} async-done(((bf16[768,3072]{1,0:T(8,128)(2,1)}), bf16[768,768]{1,0:T(8,128)(2,1)}) %reduce-scatter.2.cloned.1.call-update) | async-done | bytes 1179664 | tf_op jit(solution)/shard_map/reduce_scatter | solution.py:86
  (11 shorter events, 0.1 us)
Async XLA Ops:
  16.6 10.6 %copy-start.2 = (s32[8]{0:T(128)S(1)}, s32[8]{0:T(128)}, u32[]{:S(2)}) copy-start(s32[8]{0:T(128)} %param.8) | copy-start | bytes 100
  16.6 345.2 %all-to-all-start = ((bf16[32,96,4096]{2,1,0:T(8,128)(2,1)}), bf16[32,96,4096]{2,1,0:T(8,128)(2,1)}, u32[]{:S(2)}, u32[]{:S(2)}) async-start(bf16[32,96,4096]{2,1,0:T(8,128)(2,1)} %stack.2), calls=%async_computation | async-start | bytes 50331648 | tf_op jit(solution)/shard_map/all_to_all | solution.py:46
  26.4 503.5 %all-gather.6.cloned.1.call-start = ((), (), s32[]{:S(2)}) async-start(), calls=%async_computation.4 | async-start | bytes 4456448 | tf_op jit(solution)/shard_map/all_gather | solution.py:57
  417.8 203.6 %all-gather.4.cloned.1.call-start = ((), (), s32[]{:S(2)}) async-start(), calls=%async_computation.2 | async-start | bytes 6488064 | tf_op jit(solution)/shard_map/all_gather | solution.py:48
  418.6 264.8 %reduce-scatter.2.cloned.1.call-start = ((), (), s32[]{:S(2)}) async-start(), calls=%async_computation.3 | async-start | bytes 5898240 | tf_op jit(solution)/shard_map/reduce_scatter | solution.py:86
  438.1 94.9 %copy-start.1 = (f32[768,1,8,128]{3,2,1,0:T(8,128)S(1)}, f32[768,1,8,128]{3,2,1,0:T(8,128)}, u32[]{:S(2)}) copy-start(f32[768,1,8,128]{3,2,1,0:T(8,128)} %get-tuple-element.6) | copy-start | bytes 9437188
  533.0 8.0 %copy-start = (f32[768,1,8,128]{0,3,2,1:T(8,128)S(1)}, f32[768,1,8,128]{0,3,2,1:T(8,128)}, u32[]{:S(2)}) copy-start(f32[768,1,8,128]{0,3,2,1:T(8,128)} %copy.25) | copy-start | bytes 9437188
Sparse Core Ops, SparseCore 0:
  418.0 111.8 all-gather.5
  531.6 89.7 all-gather.3
  631.2 52.0 reduce-scatter.1
